TPU v7x, 32 devices: a whole 2x2x4 slice. The times are simulated.
32 devices in a mesh: groups: 2 (over y), atoms: 8 (over z, x), waves: 2 (over core).
Axes of the slice: x: 2, y: 2, z: 4, core: 2. Of those that a mesh axis runs over, the one named last changes fastest.
Arguments:
- features: bfloat16 [8192, 256], P(('groups', 'atoms', 'waves')), parts along dimension 0, may hold values from -6 to 6
- positions: float32 [3, 8192], P(None, ('groups', 'atoms', 'waves')), parts along dimension 1, may hold values from 0 to 1, as said below
- distances: float32 [8192, 768], P(('groups', 'atoms', 'waves')), parts along dimension 0, may hold values from 0.5 to 5
- pair_mask: int32 [8192, 768], P(('groups', 'atoms', 'waves')), parts along dimension 0, may hold values 0 or 1
- counts: int32 [32], P(('groups', 'atoms', 'waves')), parts along dimension 0, may hold values from 128 to 256, as said below
- wave_index: int32 [3, 2048], P(None, ('groups', 'waves')), parts along dimension 1, may hold values from -6 to 6
- w_value: bfloat16 [256, 256], replicated, may hold values from -0.375 to 0.375
- filter_short: float32 [16, 256], replicated, may hold values from -1 to 1
- filter_long: float32 [16, 256], replicated, may hold values from -6 to 6
- gain: float32 [256], replicated, may hold values from 0.1 to 1.9
- w_inner: bfloat16 [256, 256], replicated, may hold values from -0.375 to 0.375
- w_outer: bfloat16 [256, 256], replicated, may hold values from -0.375 to 0.375
Outputs:
- updated: bfloat16 [8192, 256], P(('groups', 'atoms', 'waves')), parts along dimension 0
There are 2 independent parts, one for each index of `groups`. A program takes and returns all parts, laid end to end along the dimension named above; an argument that names none is the same for every part. Nothing has to cross between parts.
Inputs may be any that keep to these rules, and one draw needn't show every extreme that they name: The atoms of box b are its first counts[b] slots; in every draw some box is full. `positions`: fractional coordinates; the first coordinate of every slot of box b lies in [b / 16, (b + 1) / 16).
All inputs are finite; a program needn't handle non-finite values. No bound on the sum of `pair_mask` on one device may be relied on, other than what follows from the above.
Results may differ from a plain program's by a relative error of at most 0.015.
Values may be sent and summed in bfloat16 or wider, within the bound.
A program may use at most 64 MiB of HBM per device.

v0:
```python
import jax
import jax.numpy as jnp
from jax import lax
from jax.sharding import PartitionSpec as P

radius_cut = 5.0
wave_top = 6.0 * 3.0**0.5


def padded(block, sides, width):
    for axis, dim in sides:
        count = lax.axis_size(axis)
        forward = [(i, i + 1) for i in range(count - 1)]
        forward.append((count - 1, 0))
        backward = [(target, source) for source, target in forward]
        low = lax.ppermute(
            lax.slice_in_dim(block, block.shape[dim] - width, None, axis=dim), axis, forward
        )
        high = lax.ppermute(lax.slice_in_dim(block, 0, width, axis=dim), axis, backward)
        block = jnp.concatenate([low, block, high], axis=dim)
    return block


def radial_tiles(distances, pair_mask, radial_count):
    centres = radius_cut * jnp.arange(radial_count, dtype=jnp.float32) / (radial_count - 1)
    spacing = radius_cut / (radial_count - 1)
    envelope = (
        0.5 * (jnp.cos(jnp.pi * distances / radius_cut) + 1.0) * pair_mask.astype(jnp.float32)
    )
    offsets = (distances[None] - centres[:, None, None]) / spacing
    tiles = jnp.exp(-0.5 * offsets * offsets) * envelope[None]
    return tiles.astype(jnp.bfloat16)


def phase_tiles(points, wave_index):
    waves = wave_index.astype(jnp.float32)
    theta = points[0][:, None] * waves[0][None, :] + points[1][:, None] * waves[1][None, :]
    theta = 2.0 * jnp.pi * (theta + points[2][:, None] * waves[2][None, :])
    return (jnp.cos(theta).astype(jnp.bfloat16), jnp.sin(theta).astype(jnp.bfloat16))


def wave_filter(wave_index, filter_long):
    waves = wave_index.astype(jnp.float32)
    radial_count = filter_long.shape[0]
    magnitude = jnp.sqrt(waves[0] * waves[0] + waves[1] * waves[1] + waves[2] * waves[2])
    centres = wave_top * jnp.arange(radial_count, dtype=jnp.float32) / (radial_count - 1)
    spacing = wave_top / (radial_count - 1)
    offsets = (magnitude[None, :] - centres[:, None]) / spacing
    k_basis = jnp.exp(-0.5 * offsets * offsets)
    return jnp.dot(k_basis.T, filter_long, precision=lax.Precision.HIGHEST)


def body(
    features,
    positions,
    distances,
    pair_mask,
    counts,
    wave_index,
    w_value,
    filter_short,
    filter_long,
    gain,
    w_inner,
    w_outer,
):
    row_count = features.shape[0]
    width = features.shape[1]
    radial_count = filter_short.shape[0]
    occupied = (lax.iota(jnp.int32, row_count) < counts[0]).astype(jnp.float32)
    values = (
        jnp.dot(features, w_value, preferred_element_type=jnp.float32) * occupied[:, None]
    ).astype(jnp.bfloat16)
    beside_all = padded(values, ((("atoms", "waves"), 0),), row_count)
    tiles = radial_tiles(distances, pair_mask, radial_count).reshape(
        radial_count * row_count, 3 * row_count
    )
    products = jnp.dot(tiles, beside_all, preferred_element_type=jnp.float32).reshape(
        radial_count, row_count, width
    )
    near_field = jnp.sum(products * filter_short[:, None, :], axis=0)
    wide_values, block_points = (
        lax.all_gather(values.astype(jnp.float32), "waves", axis=0, tiled=True),
        lax.all_gather(positions, "waves", axis=1, tiled=True),
    )
    block_values = wide_values.astype(jnp.bfloat16)
    cosine, sine = phase_tiles(block_points, wave_index)
    cos_sum = jnp.einsum("ak,af->kf", cosine, block_values, preferred_element_type=jnp.float32)
    sin_sum = jnp.einsum("ak,af->kf", sine, block_values, preferred_element_type=jnp.float32)
    atom_total = row_count * lax.axis_size(("atoms", "waves"))
    wave_total = wave_index.shape[1] * lax.axis_size("waves")
    factor_scale = float(atom_total) ** (-0.5)
    cos_total, sin_total = lax.psum((cos_sum, sin_sum), "atoms")
    block_filter = wave_filter(wave_index, filter_long)
    cos_filtered = (cos_total * block_filter * factor_scale).astype(jnp.bfloat16)
    sin_filtered = (sin_total * block_filter * factor_scale).astype(jnp.bfloat16)
    far_field = lax.psum_scatter(
        (
            jnp.dot(cosine, cos_filtered, preferred_element_type=jnp.float32)
            + jnp.dot(sine, sin_filtered, preferred_element_type=jnp.float32)
        ).astype(jnp.bfloat16),
        "waves",
        scatter_dimension=0,
        tiled=True,
    ).astype(jnp.float32) * float(wave_total) ** (-0.5)
    combined = features.astype(jnp.float32) + near_field + far_field
    normed = (
        combined * lax.rsqrt(jnp.mean(combined * combined, axis=-1, keepdims=True) + 1e-06) * gain
    ).astype(jnp.bfloat16)
    inner = jax.nn.silu(jnp.dot(normed, w_inner, preferred_element_type=jnp.float32)).astype(
        jnp.bfloat16
    )
    result = jnp.dot(inner, w_outer, preferred_element_type=jnp.float32) * occupied[:, None]
    return result.astype(jnp.bfloat16)


def solution(mesh):
    placed = (
        P(("groups", "atoms", "waves"), None),
        P(None, ("groups", "atoms", "waves")),
        P(("groups", "atoms", "waves"), None),
        P(("groups", "atoms", "waves"), None),
        P(("groups", "atoms", "waves")),
        P(None, ("groups", "waves")),
        P(),
        P(),
        P(),
        P(),
        P(),
        P(),
    )
    return jax.shard_map(
        body,
        mesh=mesh,
        in_specs=placed,
        out_specs=P(("groups", "atoms", "waves"), None),
        check_vma=False,
    )
```

profile of v0, /device:TPU:17, one launch (start us, length us, event | category | flops | bytes accessed | tf_op | source)
XLA Modules:
  0.0 130.0 jit_solution(18217226336184944433)
XLA Ops:
  6.5 0.0 copy-start
  6.5 0.0 copy-start.5
  6.5 0.0 all-reduce.3.cloned.1.call-start
  6.5 0.7 convert_element_type.63
  8.0 0.0 copy-done
  8.0 1.1 fusion.14
  9.1 2.3 %all_gather.7 = bf16[512,256]{1,0:T(8,128)(2,1)S(1)} all-gather(bf16[256,256]{1,0:T(8,128)(2,1)S(1)} %fusion.14), channel_id=1, replica_groups=mesh['groups'=2,'atoms'=8,'waves'=2] {'waves'}, dimensions={0}, use_global_device_ids=true | all-gather | bytes 393216 | tf_op jit(solution)/shard_map/all_gather | solution.py:83
  11.4 0.0 copy-done.5
  11.4 1.8 %all_gather.6 = f32[3,512]{1,0:T(4,128)S(1)} all-gather(f32[3,256]{1,0:T(4,128)S(1)} %copy-done.5), channel_id=1, replica_groups=mesh['groups'=2,'atoms'=8,'waves'=2] {'waves'}, dimensions={1}, use_global_device_ids=true | all-gather | bytes 9216 | tf_op jit(solution)/shard_map/all_gather | solution.py:84
  13.2 4.8 %fusion.20 = f32[512,256]{1,0:T(8,128)} fusion(f32[512]{0:T(512)S(1)} %bitcast.20, f32[512]{0:T(512)S(1)} %bitcast.36, f32[512]{0:T(512)S(1)} %bitcast.24, f32[512]{0:T(512)S(1)} %bitcast.40, f32[512]{0:T(512)S(1)} %bitcast.28, f32[512]{0:T(512)S(1)} %bitcast.32, bf16[512,256]{1,0:T(8,128)(2,1)S(1)} %all_gather.7), kind=kOutput, calls=%fused_computation.30 | convolution fusion | flops 136052736 | bytes 798720 | tf_op jit(solution)/shard_map/ak,af->kf/dot_general | solution.py:89
  18.1 4.8 %fusion.22 = f32[512,256]{1,0:T(8,128)} fusion(f32[512]{0:T(512)S(1)} %bitcast.21, f32[512]{0:T(512)S(1)} %bitcast.37, f32[512]{0:T(512)S(1)} %bitcast.25, f32[512]{0:T(512)S(1)} %bitcast.41, f32[512]{0:T(512)S(1)} %bitcast.29, f32[512]{0:T(512)S(1)} %bitcast.33, bf16[512,256]{1,0:T(8,128)(2,1)S(1)} %all_gather.7), kind=kOutput, calls=%fused_computation.32 | convolution fusion | flops 136052736 | bytes 798720 | tf_op jit(solution)/shard_map/ak,af->kf/dot_general | solution.py:88
  22.9 0.0 copy-start.4
  22.9 0.0 copy-start.1
  22.9 0.0 copy-start.2
  22.9 0.0 all-reduce.3.cloned.1.call-update
  22.9 0.0 reduce-scatter.2.cloned.1.call-start
  23.0 1.5 %collective-permute-start = (bf16[256,256]{1,0:T(8,128)(2,1)S(1)}, bf16[256,256]{1,0:T(8,128)(2,1)S(1)}, u32[]{:S(2)}, u32[]{:S(2)}) collective-permute-start(bf16[256,256]{1,0:T(8,128)(2,1)S(1)} %fusion.14), channel_id=1, source_target_pairs={{0,1},{1,2},{2,3},{3,4},{4,5},{5,6},{6,7},{7,8},{8,9},{9,10},{10,1... | collective-permute-start | bytes 393224 | tf_op jit(solution)/shard_map/ppermute | solution.py:16
  24.4 0.0 collective-permute-start.1
  24.4 0.0 copy-done.4
  24.5 0.7 fusion.35
  25.2 0.0 copy-done.1
  25.2 0.0 copy-done.2
  25.2 2.7 %convert_multiply_fusion = f32[256,768]{1,0:T(8,128)S(1)} fusion(s32[256,768]{1,0:T(8,128)S(1)} %copy-done.1, f32[256,768]{1,0:T(8,128)S(1)} %copy-done.2), kind=kLoop, calls=%fused_computation.22 | loop fusion | flops 983040 | bytes 2359296 | tf_op jit(solution)/shard_map/mul | solution.py:28
  27.9 72.7 %all-reduce.3.cloned.1.call-done = (f32[512,256]{1,0:T(8,128)}, f32[512,256]{1,0:T(8,128)}) async-done(((f32[512,256]{1,0:T(8,128)}, f32[512,256]{1,0:T(8,128)}), (f32[512,256]{1,0:T(8,128)}, f32[512,256]{1,0:T(8,128)})) %all-reduce.3.cloned.1.call-update) | async-done | bytes 1048592 | tf_op jit(solution)/shard_map/psum | solution.py:93
  100.5 0.0 copy-start.6
  100.5 5.0 %fusion.21 = f32[512,256]{1,0:T(8,128)S(1)} fusion(f32[512]{0:T(512)S(1)} %bitcast.22, f32[512]{0:T(512)S(1)} %bitcast.38, f32[512]{0:T(512)S(1)} %bitcast.26, f32[512]{0:T(512)S(1)} %bitcast.42, f32[512]{0:T(512)S(1)} %bitcast.30, f32[512]{0:T(512)S(1)} %bitcast.34, f32[512,256]{1,0:T(8,128)} %get-tuple-element.5, f32[512,256]{1,0:T(8,128)S(1)} %fusion.35), kind=kOutput, calls=%fused_computation.31 | convolution fusion | flops 136445952 | bytes 1585152 | tf_op jit(solution)/shard_map/dot_general | solution.py:99
  105.5 0.0 copy-done.6
  105.5 0.0 copy-start.9
  105.6 4.9 %fusion.13 = bf16[512,256]{1,0:T(8,128)(2,1)} fusion(f32[512,256]{1,0:T(8,128)S(1)} %fusion.21, f32[512]{0:T(512)S(1)} %bitcast.23, f32[512]{0:T(512)S(1)} %bitcast.39, f32[512]{0:T(512)S(1)} %bitcast.27, f32[512]{0:T(512)S(1)} %bitcast.43, f32[512]{0:T(512)S(1)} %bitcast.31, f32[512]{0:T(512)S(1)} %bitcast.35, f32[512,256]{1,0:T(8,128)S(1)} %copy-done.6, ...), kind=kOutput, calls=%fused_computation.14 | convolution fusion | flops 136708096 | bytes 1847296 | tf_op jit(solution)/shard_map/dot_general | solution.py:100
  110.5 0.0 reduce-scatter.2.cloned.1.call-update
  110.5 0.0 copy-start.3
  110.5 0.0 copy-start.7
  110.5 0.0 copy-start.8
  110.5 0.0 copy-start.10
  110.6 0.0 collective-permute-done
  110.6 0.0 collective-permute-done.1
  110.6 0.0 copy-done.9
  110.6 3.9 %multiply_reduce_fusion = f32[256,256]{1,0:T(8,128)S(1)} fusion(f32[16,256]{1,0:T(8,128)S(1)} %copy-done.9, f32[256,768]{1,0:T(8,128)S(1)} %convert_multiply_fusion, f32[16]{0:T(128)S(1)} %iota_multiply_fusion.1, f32[256,768]{1,0:T(8,128)S(1)} %copy-done.2, bf16[256,256]{1,0:T(8,128)(2,1)S(1)} %collective-permute-done.1, bf16[256,256]{1,0:T(8,128)(2,1)S(1)} %fusion.14, ...), kind=kOutput, calls=%fused_computation.12 | convolution fusion | flops 1632698368 | bytes 2244672 | tf_op jit(solution)/shard_map/dot_general | solution.py:78
  114.4 5.6 %reduce-scatter.2.cloned.1.call-done = bf16[256,256]{1,0:T(8,128)(2,1)} async-done(((bf16[512,256]{1,0:T(8,128)(2,1)}), bf16[256,256]{1,0:T(8,128)(2,1)}) %reduce-scatter.2.cloned.1.call-update) | async-done | bytes 131088 | tf_op jit(solution)/shard_map/reduce_scatter | solution.py:97
  120.1 0.0 copy-done.3
  120.1 1.0 multiply_reduce_fusion.1
  121.2 0.0 copy-done.7
  121.2 0.0 copy-done.8
  121.2 0.0 copy-done.10
  121.2 2.0 %fusion.15 = bf16[256,256]{1,0:T(8,128)(2,1)} fusion(bf16[256,256]{1,0:T(8,128)(2,1)S(1)} %copy-done.7, bf16[256,256]{1,0:T(8,128)(2,1)S(1)} %copy-done.8, f32[256]{0:T(256)S(1)} %copy-done.10, f32[256]{0:T(256)S(1)} %add_rsqrt_fusion, f32[256]{0:T(256)S(1)} %compare_convert_fusion, bf16[256,256]{1,0:T(8,128)(2,1)} %reduce-scatter.2.cloned.1.call-done, ...), kind=kOutput, calls=%fused_computation.18 | convolution fusion | flops 68091904 | bytes 920576 | tf_op jit(solution)/shard_map/dot_general | solution.py:113
  (6 shorter events, 0.0 us)
Async XLA Ops:
  6.5 1.4 %copy-start = (bf16[256,256]{1,0:T(8,128)(2,1)S(1)}, bf16[256,256]{1,0:T(8,128)(2,1)}, u32[]{:S(2)}) copy-start(bf16[256,256]{1,0:T(8,128)(2,1)} %param.18) | copy-start | bytes 393220
  6.5 4.8 %copy-start.5 = (f32[3,256]{1,0:T(4,128)S(1)}, f32[3,256]{1,0:T(4,128)}, u32[]{:S(2)}) copy-start(f32[3,256]{1,0:T(4,128)} %param.13) | copy-start | bytes 9220
  6.5 94.0 %all-reduce.3.cloned.1.call-start = ((), (), s32[]{:S(2)}) async-start(), calls=%async_computation.2 | async-start | bytes 2097152 | tf_op jit(solution)/shard_map/psum | solution.py:93
  22.9 1.6 %copy-start.4 = (f32[16,256]{1,0:T(8,128)S(1)}, f32[16,256]{1,0:T(8,128)}, u32[]{:S(2)}) copy-start(f32[16,256]{1,0:T(8,128)} %param.20) | copy-start | bytes 49156
  22.9 2.3 %copy-start.1 = (s32[256,768]{1,0:T(8,128)S(1)}, s32[256,768]{1,0:T(8,128)}, u32[]{:S(2)}) copy-start(s32[256,768]{1,0:T(8,128)} %param.15) | copy-start | bytes 2359300
  22.9 2.3 %copy-start.2 = (f32[256,768]{1,0:T(8,128)S(1)}, f32[256,768]{1,0:T(8,128)}, u32[]{:S(2)}) copy-start(f32[256,768]{1,0:T(8,128)} %param.14) | copy-start | bytes 2359300
  22.9 97.2 %reduce-scatter.2.cloned.1.call-start = ((), (), s32[]{:S(2)}) async-start(), calls=%async_computation.1 | async-start | bytes 393216 | tf_op jit(solution)/shard_map/reduce_scatter | solution.py:97
  23.0 87.6 %collective-permute-start = (bf16[256,256]{1,0:T(8,128)(2,1)S(1)}, bf16[256,256]{1,0:T(8,128)(2,1)S(1)}, u32[]{:S(2)}, u32[]{:S(2)}) collective-permute-start(bf16[256,256]{1,0:T(8,128)(2,1)S(1)} %fusion.14), channel_id=1, source_target_pairs={{0,1},{1,2},{2,3},{3,4},{4,5},{5,6},{6,7},{7,8},{8,9},{9,10},{10,1... | collective-permute-start | bytes 393224 | tf_op jit(solution)/shard_map/ppermute | solution.py:16
  24.4 86.1 %collective-permute-start.1 = (bf16[256,256]{1,0:T(8,128)(2,1)S(1)}, bf16[256,256]{1,0:T(8,128)(2,1)S(1)}, u32[]{:S(2)}, u32[]{:S(2)}) collective-permute-start(bf16[256,256]{1,0:T(8,128)(2,1)S(1)} %fusion.14), channel_id=1, source_target_pairs={{1,0},{2,1},{3,2},{4,3},{5,4},{6,5},{7,6},{8,7},{9,8},{10,9},{11,1... | collective-permute-start | bytes 393224 | tf_op jit(solution)/shard_map/ppermute | solution.py:19
  100.5 5.0 %copy-start.6 = (f32[512,256]{1,0:T(8,128)S(1)}, f32[512,256]{1,0:T(8,128)}, u32[]{:S(2)}) copy-start(f32[512,256]{1,0:T(8,128)} %get-tuple-element.6) | copy-start | bytes 1572868
  105.5 5.0 %copy-start.9 = (f32[16,256]{1,0:T(8,128)S(1)}, f32[16,256]{1,0:T(8,128)}, u32[]{:S(2)}) copy-start(f32[16,256]{1,0:T(8,128)} %param.19) | copy-start | bytes 49156
  110.5 9.6 %copy-start.3 = (bf16[256,256]{1,0:T(8,128)(2,1)S(1)}, bf16[256,256]{1,0:T(8,128)(2,1)}, u32[]{:S(2)}) copy-start(bf16[256,256]{1,0:T(8,128)(2,1)} %param.12) | copy-start | bytes 393220
  110.5 10.6 %copy-start.7 = (bf16[256,256]{1,0:T(8,128)(2,1)S(1)}, bf16[256,256]{1,0:T(8,128)(2,1)}, u32[]{:S(2)}) copy-start(bf16[256,256]{1,0:T(8,128)(2,1)} %param.23) | copy-start | bytes 393220
  110.5 10.6 %copy-start.8 = (bf16[256,256]{1,0:T(8,128)(2,1)S(1)}, bf16[256,256]{1,0:T(8,128)(2,1)}, u32[]{:S(2)}) copy-start(bf16[256,256]{1,0:T(8,128)(2,1)} %param.22) | copy-start | bytes 393220
  110.5 10.6 %copy-start.10 = (f32[256]{0:T(256)S(1)}, f32[256]{0:T(256)}, u32[]{:S(2)}) copy-start(f32[256]{0:T(256)} %param.21) | copy-start | bytes 3076
Sparse Core Ops, SparseCore 0:
  23.0 77.4 all-reduce.2
  110.6 9.4 reduce-scatter.1
where the time goes:
time: 131 us; the launch traced here: 130 us
  waiting for transfers between devices  78.3 us (60%)
  matrix products  27.2 us (21%)
  between operations  14.2 us (11%)
  other arithmetic  4.51 us (3%)
  blocking collectives  4.15 us (3%)
  starting transfers between devices  1.5 us (1%)
    psum x1, waiting for transfers between devices, body(): cos_total, sin_total = lax.psum((cos_sum, sin_sum), 'atoms')  72.7 us
    reduce_scatter x1, waiting for transfers between devices, body(): lax.psum_scatter((jnp.dot(cosine, cos_filtered, preferred_element_type=jn...  5.65 us
    dot_general x1, matrix products, body(): jnp.dot(cosine, cos_filtered, preferred_element_type=jnp.float32)  4.99 us
    dot_general x1, matrix products, body(): jnp.dot(sine, sin_filtered, preferred_element_type=jnp.float32)  4.93 us
    dot_general x1, matrix products, body(): jnp.einsum('ak,af->kf', sine, block_values, preferred_element_type=jnp.fl...  4.83 us
    dot_general x1, matrix products, body(): jnp.einsum('ak,af->kf', cosine, block_values, preferred_element_type=jnp....  4.82 us
    dot_general x1, matrix products, body(): jnp.dot(tiles, beside_all, preferred_element_type=jnp.float32)  3.85 us
    mul x1, other arithmetic, radial_tiles(): 0.5 * (jnp.cos(jnp.pi * distances / radius_cut) + 1.0)  2.69 us
  transfers between devices with their start and end apart: 4, of which 2 were waited for; matrix products, arithmetic and copies ran while one was open for 13% of the time, Pallas kernels for 0%

commit v1 on v0

--- a/solution.py
+++ b/solution.py
@@ -1,6 +1,11 @@
+import functools
+import math
+
 import jax
 import jax.numpy as jnp
 from jax import lax
+from jax.experimental import pallas as pl
+from jax.experimental.pallas import tpu as pltpu
 from jax.sharding import PartitionSpec as P
 
 radius_cut = 5.0
@@ -50,7 +55,7 @@
     return jnp.dot(k_basis.T, filter_long, precision=lax.Precision.HIGHEST)
 
 
-def body(
+def collective_body(
     features,
     positions,
     distances,
@@ -114,6 +119,416 @@
     return result.astype(jnp.bfloat16)
 
 
+MESH = pl.DeviceIdType.MESH
+cos_terms = (
+    0.9999999890590217,
+    -19.73920449945381,
+    64.93911745989173,
+    -85.45013953082398,
+    60.16763095051855,
+    -25.967599246994247,
+    6.528658159389057,
+)
+sin_terms = (
+    6.283184916495431,
+    -41.34158923268848,
+    81.59994332978006,
+    -76.61447253122435,
+    41.34288235446963,
+    -12.471243534886277,
+)
+
+
+def horner(square, terms):
+    total = square * terms[-1] + terms[-2]
+    for term in terms[-3::-1]:
+        total = total * square + term
+    return total
+
+
+def turned(turns):
+    part = turns - jnp.floor(turns + 0.5)
+    square = part * part
+    return horner(square, cos_terms), part * horner(square, sin_terms)
+
+
+def split_of(count):
+    low = 1
+    for size in range(1, count + 1):
+        if count % size == 0 and size * size <= count:
+            low = size
+    return low, count // low
+
+
+def kernel(
+    low_count,
+    high_count,
+    features,
+    positions,
+    distances,
+    pair_mask,
+    counts,
+    wave_index,
+    w_value,
+    filter_short,
+    filter_long,
+    gain,
+    w_inner,
+    w_outer,
+    updated,
+    dist,
+    mask,
+    values,
+    points,
+    waves,
+    wave_cols,
+    phases,
+    phases_t,
+    own_sums,
+    low_out,
+    low_in,
+    high_out,
+    high_in,
+    filtered,
+    block_filter,
+    envelope,
+    tiles,
+    near,
+    far_out,
+    far_in,
+    load_sem,
+    pair_send,
+    pair_recv,
+    low_send,
+    low_recv,
+    high_send,
+    high_recv,
+    spread_send,
+    spread_recv,
+    relay_send,
+    relay_recv,
+):
+    rows = features.shape[0]
+    radial_count = filter_short.shape[0]
+    wave_count = wave_index.shape[1]
+    atoms_count = low_count * high_count
+    chunk = wave_count // atoms_count
+    a = lax.axis_index("atoms")
+    w = lax.axis_index("waves")
+    high, low = a // low_count, a % low_count
+    partner = {"atoms": a, "waves": 1 - w}
+    other = {"atoms": (a + 2 * w - 1 + atoms_count) % atoms_count, "waves": 1 - w}
+
+    def low_peer(step):
+        return {"atoms": high * low_count + (low + step) % low_count, "waves": w}
+
+    def high_peer(step):
+        return {"atoms": ((high + step) % high_count) * low_count + low, "waves": w}
+
+    peers = [partner, other]
+    peers += [low_peer(step) for step in range(1, low_count)]
+    peers += [high_peer(step) for step in range(1, high_count)]
+
+    load_dist = pltpu.make_async_copy(distances, dist, load_sem.at[0])
+    load_mask = pltpu.make_async_copy(pair_mask, mask, load_sem.at[1])
+    load_dist.start()
+    load_mask.start()
+    barrier = pltpu.get_barrier_semaphore()
+    for peer in peers:
+        pl.semaphore_signal(barrier, inc=1, device_id=peer, device_id_type=MESH)
+
+    def remote(src, dst, send, recv, peer):
+        copy = pltpu.make_async_remote_copy(
+            src_ref=src,
+            dst_ref=dst,
+            send_sem=send,
+            recv_sem=recv,
+            device_id=peer,
+            device_id_type=MESH,
+        )
+        copy.start()
+        return copy
+
+    occupied = (lax.broadcasted_iota(jnp.int32, (rows, 1), 0) < counts[0]).astype(jnp.float32)
+    values[1] = (
+        jnp.dot(features[...], w_value[...], preferred_element_type=jnp.float32) * occupied
+    ).astype(jnp.bfloat16)
+    points[0] = positions[...]
+    waves[...] = jnp.zeros_like(waves)
+    waves[0:3, :] = wave_index[...].astype(jnp.float32)
+    pl.semaphore_wait(barrier, len(peers))
+
+    started = []
+    points_copy = remote(points.at[0], points.at[1], pair_send.at[0], pair_recv.at[0], partner)
+    pair_copy = remote(
+        values.at[1], values.at[2 * w], pair_send.at[1], pair_recv.at[1], partner
+    )
+    other_copy = remote(
+        values.at[1], values.at[2 - 2 * w], pair_send.at[2], pair_recv.at[2], other
+    )
+    started += [points_copy, pair_copy, other_copy]
+
+    wave = waves[...]
+    magnitude = jnp.sqrt(
+        wave[0:1] * wave[0:1] + wave[1:2] * wave[1:2] + wave[2:3] * wave[2:3]
+    )
+    spacing = wave_top / (radial_count - 1)
+    centres = lax.broadcasted_iota(jnp.int32, (radial_count, 1), 0).astype(jnp.float32) * spacing
+    offsets = (magnitude - centres) / spacing
+    k_basis = jnp.exp(-0.5 * offsets * offsets)
+    block_filter[...] = lax.dot_general(
+        k_basis,
+        filter_long[...],
+        (((0,), (0,)), ((), ())),
+        precision=lax.Precision.HIGHEST,
+        preferred_element_type=jnp.float32,
+    ) * (float(rows * 2 * atoms_count) ** -0.5)
+    wave_t = wave.T
+
+    points_copy.wait_recv()
+    point_rows = jnp.concatenate([points[0], points[1]], axis=1)
+
+    order = sorted(range(high_count), key=lambda e: (e == 0, abs(2 * e - high_count)))
+
+    wave_cols[...] = wave_t
+
+    def chunk_sums(index):
+        begin = pl.multiple_of(index * chunk, chunk)
+        base = pl.multiple_of(index * 2 * chunk, 2 * chunk)
+        cols = wave_cols[pl.ds(begin, chunk), :]
+        turns = cols[:, 0:1] * point_rows[0:1] + cols[:, 1:2] * point_rows[1:2]
+        turns = turns + cols[:, 2:3] * point_rows[2:3]
+        cosine, sine = turned(turns)
+        phases[pl.ds(base, chunk), :] = cosine.astype(jnp.bfloat16)
+        phases[pl.ds(base + chunk, chunk), :] = sine.astype(jnp.bfloat16)
+        block = phases[pl.ds(base, 2 * chunk), :]
+        return jnp.dot(
+            block[:, 0:rows], values[1], preferred_element_type=jnp.float32
+        ) + jnp.dot(
+            block[:, rows : 2 * rows], values[2 - 2 * w], preferred_element_type=jnp.float32
+        )
+
+    first = True
+    low_copies = {}
+    for step in range(1, low_count):
+        for e in order:
+            index = ((high + e) % high_count) * low_count + (low + step) % low_count
+            if first:
+                pair_copy.wait_recv()
+                first = False
+            low_out[step - 1, e] = chunk_sums(index).astype(jnp.bfloat16)
+            low_copies[step, e] = remote(
+                low_out.at[step - 1, e],
+                low_in.at[step - 1, e],
+                low_send.at[step - 1, e],
+                low_recv.at[step - 1, e],
+                low_peer(step),
+            )
+            started.append(low_copies[step, e])
+    for e in order:
+        own_sums[e] = chunk_sums(((high + e) % high_count) * low_count + low)
+
+    load_dist.wait()
+    load_mask.wait()
+    turns = dist[...] * (0.5 / radius_cut)
+    part = turns - jnp.floor(turns + 0.5)
+    envelope[...] = (0.5 * horner(part * part, cos_terms) + 0.5) * mask[...].astype(jnp.float32)
+    near[...] = jnp.zeros_like(near)
+    other_copy.wait_recv()
+    sharp = math.sqrt(0.5 * math.log2(math.e)) * (radial_count - 1) / radius_cut
+    shift = radius_cut / (radial_count - 1)
+
+    def near_pair(k2, carry):
+        for half in range(2):
+            k = k2 * 2 + half
+            offset = (dist[...] - k.astype(jnp.float32) * shift) * sharp
+            tiles[half * rows : (half + 1) * rows, :] = (
+                jnp.exp2(-(offset * offset)) * envelope[...]
+            ).astype(jnp.bfloat16)
+        beside = values[...].reshape(3 * rows, values.shape[2])
+        products = jnp.dot(tiles[...], beside, preferred_element_type=jnp.float32)
+        near[...] += (
+            products[0:rows] * filter_short[pl.ds(k2 * 2, 1), :]
+            + products[rows : 2 * rows] * filter_short[pl.ds(k2 * 2 + 1, 1), :]
+        )
+        return carry
+
+    pairs = radial_count // 2
+    done = 0
+
+    def near_until(stop):
+        nonlocal done
+        if stop > done:
+            lax.fori_loop(done, stop, near_pair, 0)
+            done = stop
+
+    high_copies = {}
+    for place, e in enumerate(order):
+        near_until(min(pairs, place + 1))
+        total = own_sums[e]
+        for step in range(1, low_count):
+            low_copies[step, e].wait_recv()
+            total = total + low_in[step - 1, e].astype(jnp.float32)
+        if e == 0:
+            own_sums[0] = total
+        else:
+            high_out[e - 1] = total.astype(jnp.bfloat16)
+            high_copies[e] = remote(
+                high_out.at[e - 1],
+                high_in.at[e - 1],
+                high_send.at[e - 1],
+                high_recv.at[e - 1],
+                high_peer(e),
+            )
+            started.append(high_copies[e])
+
+    near_until(min(pairs, high_count + 2))
+    total = own_sums[0]
+    for e in range(1, high_count):
+        high_copies[e].wait_recv()
+        total = total + high_in[e - 1].astype(jnp.float32)
+    own_filter = block_filter[pl.ds(pl.multiple_of(a * chunk, chunk), chunk), :]
+
+    def chunk_rows(index):
+        return pl.ds(pl.multiple_of(index * 2 * chunk, 2 * chunk), 2 * chunk)
+
+    own_rows = chunk_rows(a)
+    filtered[own_rows, :] = (total * jnp.concatenate([own_filter, own_filter], axis=0)).astype(
+        jnp.bfloat16
+    )
+    spread = {}
+    for e in order:
+        if e:
+            spread[e] = remote(
+                filtered.at[own_rows],
+                filtered.at[own_rows],
+                spread_send.at[e - 1],
+                spread_recv.at[e - 1],
+                high_peer(e),
+            )
+            started.append(spread[e])
+    relay = []
+
+    def pass_on(e):
+        source = ((high - e + high_count) % high_count) * low_count + low
+        for step in range(1, low_count):
+            copy = remote(
+                filtered.at[chunk_rows(source)],
+                filtered.at[chunk_rows(source)],
+                relay_send.at[step - 1, e],
+                relay_recv.at[step - 1, e],
+                low_peer(step),
+            )
+            relay.append(copy)
+            started.append(copy)
+
+    pass_on(0)
+    near_until(pairs)
+    phases_t[...] = phases[...].T
+    for e in sorted(range(1, high_count), key=lambda e: -abs(2 * e - high_count)):
+        spread[e].wait_recv()
+        pass_on(e)
+    for copy in relay:
+        copy.wait_recv()
+
+    far_out[...] = jnp.dot(
+        phases_t[rows : 2 * rows, :], filtered[...], preferred_element_type=jnp.float32
+    ).astype(jnp.bfloat16)
+    far_copy = remote(far_out, far_in, pair_send.at[3], pair_recv.at[3], partner)
+    started.append(far_copy)
+    own_far = jnp.dot(phases_t[0:rows, :], filtered[...], preferred_element_type=jnp.float32)
+    combined = features[...].astype(jnp.float32) + near[...]
+    far_copy.wait_recv()
+    far_field = (own_far + far_in[...].astype(jnp.float32)) * (float(2 * wave_count) ** -0.5)
+    combined = combined + far_field
+    normed = (
+        combined
+        * lax.rsqrt(jnp.mean(combined * combined, axis=-1, keepdims=True) + 1e-06)
+        * gain[...]
+    ).astype(jnp.bfloat16)
+    inner = jnp.dot(normed, w_inner[...], preferred_element_type=jnp.float32)
+    inner = (inner / (1.0 + jnp.exp(-inner))).astype(jnp.bfloat16)
+    result = jnp.dot(inner, w_outer[...], preferred_element_type=jnp.float32) * occupied
+    updated[...] = result.astype(jnp.bfloat16)
+    for copy in started:
+        copy.wait_send()
+
+
+def kernel_body(low_count, high_count, features, positions, distances, pair_mask, counts,
+                wave_index, w_value, filter_short, filter_long, gain, w_inner, w_outer):
+    rows, width = features.shape
+    wave_count = wave_index.shape[1]
+    atoms_count = low_count * high_count
+    chunk2 = 2 * wave_count // atoms_count
+    columns = distances.shape[1]
+    bf16, f32 = jnp.bfloat16, jnp.float32
+    vmem = pl.BlockSpec(memory_space=pltpu.VMEM)
+    hbm = pl.BlockSpec(memory_space=pl.ANY)
+    smem = pl.BlockSpec(memory_space=pltpu.SMEM)
+    dma = pltpu.SemaphoreType.DMA
+    return pl.pallas_call(
+        functools.partial(kernel, low_count, high_count),
+        out_shape=jax.ShapeDtypeStruct((rows, width), bf16),
+        in_specs=[vmem, vmem, hbm, hbm, smem] + [vmem] * 7,
+        out_specs=vmem,
+        scratch_shapes=[
+            pltpu.VMEM((rows, columns), f32),
+            pltpu.VMEM((rows, columns), jnp.int32),
+            pltpu.VMEM((3, rows, width), bf16),
+            pltpu.VMEM((2, 3, rows), f32),
+            pltpu.VMEM((8, wave_count), f32),
+            pltpu.VMEM((wave_count, 8), f32),
+            pltpu.VMEM((2 * wave_count, 2 * rows), bf16),
+            pltpu.VMEM((2 * rows, 2 * wave_count), bf16),
+            pltpu.VMEM((high_count, chunk2, width), f32),
+            pltpu.VMEM((low_count - 1, high_count, chunk2, width), bf16),
+            pltpu.VMEM((low_count - 1, high_count, chunk2, width), bf16),
+            pltpu.VMEM((high_count - 1, chunk2, width), bf16),
+            pltpu.VMEM((high_count - 1, chunk2, width), bf16),
+            pltpu.VMEM((2 * wave_count, width), bf16),
+            pltpu.VMEM((wave_count, width), f32),
+            pltpu.VMEM((rows, columns), f32),
+            pltpu.VMEM((2 * rows, columns), bf16),
+            pltpu.VMEM((rows, width), f32),
+            pltpu.VMEM((rows, width), bf16),
+            pltpu.VMEM((rows, width), bf16),
+            dma((2,)),
+            dma((4,)),
+            dma((4,)),
+            dma((low_count - 1, high_count)),
+            dma((low_count - 1, high_count)),
+            dma((high_count - 1,)),
+            dma((high_count - 1,)),
+            dma((high_count - 1,)),
+            dma((high_count - 1,)),
+            dma((low_count - 1, high_count)),
+            dma((low_count - 1, high_count)),
+        ],
+        compiler_params=pltpu.CompilerParams(
+            collective_id=0, has_side_effects=True, vmem_limit_bytes=40 * 1024 * 1024
+        ),
+        cost_estimate=pl.CostEstimate(
+            flops=2 * rows * columns * width * filter_short.shape[0],
+            bytes_accessed=8 * rows * columns,
+            transcendentals=rows * columns * filter_short.shape[0],
+        ),
+    )(features, positions, distances, pair_mask, counts, wave_index, w_value, filter_short,
+      filter_long, gain.reshape(1, width), w_inner, w_outer)
+
+
+def body_for(mesh):
+    atoms_count = mesh.shape["atoms"]
+    low_count, high_count = split_of(atoms_count)
+
+    def body(*arrays):
+        chunk = arrays[5].shape[1] // atoms_count
+        if low_count > 1 and chunk % 16 == 0 and arrays[5].shape[1] % atoms_count == 0:
+            return kernel_body(low_count, high_count, *arrays)
+        return collective_body(*arrays)
+
+    return body
+
+
 def solution(mesh):
     placed = (
         P(("groups", "atoms", "waves"), None),
@@ -130,7 +545,7 @@
         P(),
     )
     return jax.shard_map(
-        body,
+        body_for(mesh),
         mesh=mesh,
         in_specs=placed,
         out_specs=P(("groups", "atoms", "waves"), None),

time: 131 us -> 43.3 us (0.33)
  waiting for transfers between devices: 78.3 us -> 0 us
  Pallas kernels: 0 us -> 32.1 us
  matrix products: 27.2 us -> 0 us
  between operations: 14.2 us -> 0.68 us
  local copies, waits for them, and re-layouts: 0.06 us -> 10 us
  other arithmetic: 4.51 us -> 0 us
  blocking collectives: 4.15 us -> 0 us
  starting transfers between devices: 1.5 us -> 0 us
    psum x1 -> x0, waiting for transfers between devices: 72.7 us -> none  [body(): cos_total, sin_total = lax.psum((cos_sum, sin_sum), 'atoms')]
    pallas_call x0 -> x1, Pallas kernels: none -> 32.1 us  [kernel_body(): pl.pallas_call(functools.partial(kernel, low_count, high_count), out_shap...]
    dot_general x8 -> x0, matrix products: 27.2 us -> none  [the longest x1 4.99 us: body(): jnp.dot(cosine, cos_filtered, preferred_element_type=jnp.float32)]
    unnamed x22 -> x23, local copies, waits for them, and re-layouts: 0.06 us -> 10 us
    reduce_scatter x1 -> x0, waiting for transfers between devices: 5.65 us -> none  [body(): lax.psum_scatter((jnp.dot(cosine, cos_filtered, preferred_element_type=jn...]
    all_gather x2 -> x0, blocking collectives: 4.15 us -> none  [the longest x1 2.31 us: body(): lax.all_gather(values.astype(jnp.float32), 'waves', axis=0, tiled=True)]
    mul x1 -> x0, other arithmetic: 2.69 us -> none  [radial_tiles(): 0.5 * (jnp.cos(jnp.pi * distances / radius_cut) + 1.0)]
    ppermute x2 -> x0, starting transfers between devices: 1.46 us -> none  [the longest x1 1.46 us: padded(): lax.ppermute(lax.slice_in_dim(block, block.shape[dim] - width, None, axis...]
  transfers between devices with their start and end apart: 4 -> 0, of which waited for: 2 -> 0; matrix products, arithmetic and copies ran while one was open for 13% -> 0% of each run, Pallas kernels for 0% -> 0%
where the time goes in v1:
time: 43.3 us; the launch traced here: 42.8 us
  Pallas kernels  32.1 us (74%)
  local copies, waits for them, and re-layouts  10 us (23%)
  between operations  0.68 us (2%)
    pallas_call x1, Pallas kernels, kernel_body(): pl.pallas_call(functools.partial(kernel, low_count, high_count), out_shap...  32.1 us
    unnamed x23, local copies, waits for them, and re-layouts  10 us

profile of v1, /device:TPU:17, one launch (start us, length us, event | category | flops | bytes accessed | tf_op | source)
XLA Modules:
  0.0 42.8 jit_solution(7834831709521506791)
XLA Ops:
  0.7 0.0 copy-start.10
  0.7 0.7 %copy-done.10 = f32[256]{0:T(256)S(1)} copy-done((f32[256]{0:T(256)S(1)}, f32[256]{0:T(256)}, u32[]{:S(2)}) %copy-start.10) | copy-done | bytes 1048
  1.3 0.0 copy-start
  1.3 1.1 %copy-done = f32[256,768]{1,0:T(8,128)S(1)} copy-done((f32[256,768]{1,0:T(8,128)S(1)}, f32[256,768]{1,0:T(8,128)}, u32[]{:S(2)}) %copy-start) | copy-done | bytes 786456
  2.5 0.0 copy-start.1
  2.5 1.1 %copy-done.1 = s32[256,768]{1,0:T(8,128)S(1)} copy-done((s32[256,768]{1,0:T(8,128)S(1)}, s32[256,768]{1,0:T(8,128)}, u32[]{:S(2)}) %copy-start.1) | copy-done | bytes 786456
  3.6 0.0 copy-start.2
  3.6 0.9 %copy-done.2 = bf16[256,256]{1,0:T(8,128)(2,1)S(1)} copy-done((bf16[256,256]{1,0:T(8,128)(2,1)S(1)}, bf16[256,256]{1,0:T(8,128)(2,1)}, u32[]{:S(2)}) %copy-start.2) | copy-done | bytes 131096
  4.5 0.0 copy-start.3
  4.5 0.9 %copy-done.3 = bf16[256,256]{1,0:T(8,128)(2,1)S(1)} copy-done((bf16[256,256]{1,0:T(8,128)(2,1)S(1)}, bf16[256,256]{1,0:T(8,128)(2,1)}, u32[]{:S(2)}) %copy-start.3) | copy-done | bytes 131096
  5.4 0.0 copy-start.4
  5.4 0.9 %copy-done.4 = bf16[256,256]{1,0:T(8,128)(2,1)S(1)} copy-done((bf16[256,256]{1,0:T(8,128)(2,1)S(1)}, bf16[256,256]{1,0:T(8,128)(2,1)}, u32[]{:S(2)}) %copy-start.4) | copy-done | bytes 131096
  6.3 0.0 copy-start.5
  6.3 0.9 %copy-done.5 = bf16[256,256]{1,0:T(8,128)(2,1)S(1)} copy-done((bf16[256,256]{1,0:T(8,128)(2,1)S(1)}, bf16[256,256]{1,0:T(8,128)(2,1)}, u32[]{:S(2)}) %copy-start.5) | copy-done | bytes 131096
  7.2 0.0 copy-start.6
  7.2 0.7 %copy-done.6 = f32[16,256]{1,0:T(8,128)S(1)} copy-done((f32[16,256]{1,0:T(8,128)S(1)}, f32[16,256]{1,0:T(8,128)}, u32[]{:S(2)}) %copy-start.6) | copy-done | bytes 16408
  7.9 0.0 copy-start.7
  7.9 0.7 %copy-done.7 = f32[16,256]{1,0:T(8,128)S(1)} copy-done((f32[16,256]{1,0:T(8,128)S(1)}, f32[16,256]{1,0:T(8,128)}, u32[]{:S(2)}) %copy-start.7) | copy-done | bytes 16408
  8.7 0.0 copy-start.8
  8.7 0.7 %copy-done.8 = s32[3,512]{1,0:T(4,128)S(1)} copy-done((s32[3,512]{1,0:T(4,128)S(1)}, s32[3,512]{1,0:T(4,128)}, u32[]{:S(2)}) %copy-start.8) | copy-done | bytes 6168
  9.4 0.0 copy-start.9
  9.4 0.7 %copy-done.9 = f32[3,256]{1,0:T(4,128)S(1)} copy-done((f32[3,256]{1,0:T(4,128)S(1)}, f32[3,256]{1,0:T(4,128)}, u32[]{:S(2)}) %copy-start.9) | copy-done | bytes 3096
  10.0 32.1 %shard_map.118 = bf16[256,256]{1,0:T(8,128)(2,1)S(1)} custom-call(bf16[256,256]{1,0:T(8,128)(2,1)S(1)} %copy-done.2, f32[3,256]{1,0:T(4,128)S(1)} %copy-done.9, f32[256,768]{1,0:T(8,128)S(1)} %copy-done, s32[256,768]{1,0:T(8,128)S(1)} %copy-done.1, s32[1]{0:T(128)S(6)} %copy.14.counts, s32[3,512]{1,0:T(4,128)S(1)} %copy-done.8, ...), custom_call_target="tpu_custom_call" | custom-call | flops 1610612736 | bytes 1572864 | tf_op jit(solution)/shard_map/pallas_call | solution.py:469
  42.2 0.7 %copy.15 = bf16[256,256]{1,0:T(8,128)(2,1)} copy(bf16[256,256]{1,0:T(8,128)(2,1)S(1)} %shard_map.118) | data formatting | bytes 262144
Async XLA Ops:
  0.7 0.7 %copy-start.10 = (f32[256]{0:T(256)S(1)}, f32[256]{0:T(256)}, u32[]{:S(2)}) copy-start(f32[256]{0:T(256)} %param.21) | copy-start | bytes 3076
  1.3 1.1 %copy-start = (f32[256,768]{1,0:T(8,128)S(1)}, f32[256,768]{1,0:T(8,128)}, u32[]{:S(2)}) copy-start(f32[256,768]{1,0:T(8,128)} %distances.1) | copy-start | bytes 2359300
  2.5 1.1 %copy-start.1 = (s32[256,768]{1,0:T(8,128)S(1)}, s32[256,768]{1,0:T(8,128)}, u32[]{:S(2)}) copy-start(s32[256,768]{1,0:T(8,128)} %pair_mask.1) | copy-start | bytes 2359300
  3.6 0.9 %copy-start.2 = (bf16[256,256]{1,0:T(8,128)(2,1)S(1)}, bf16[256,256]{1,0:T(8,128)(2,1)}, u32[]{:S(2)}) copy-start(bf16[256,256]{1,0:T(8,128)(2,1)} %features.1) | copy-start | bytes 393220
  4.5 0.9 %copy-start.3 = (bf16[256,256]{1,0:T(8,128)(2,1)S(1)}, bf16[256,256]{1,0:T(8,128)(2,1)}, u32[]{:S(2)}) copy-start(bf16[256,256]{1,0:T(8,128)(2,1)} %w_value.1) | copy-start | bytes 393220
  5.4 0.9 %copy-start.4 = (bf16[256,256]{1,0:T(8,128)(2,1)S(1)}, bf16[256,256]{1,0:T(8,128)(2,1)}, u32[]{:S(2)}) copy-start(bf16[256,256]{1,0:T(8,128)(2,1)} %w_inner.1) | copy-start | bytes 393220
  6.3 0.9 %copy-start.5 = (bf16[256,256]{1,0:T(8,128)(2,1)S(1)}, bf16[256,256]{1,0:T(8,128)(2,1)}, u32[]{:S(2)}) copy-start(bf16[256,256]{1,0:T(8,128)(2,1)} %w_outer.1) | copy-start | bytes 393220
  7.2 0.7 %copy-start.6 = (f32[16,256]{1,0:T(8,128)S(1)}, f32[16,256]{1,0:T(8,128)}, u32[]{:S(2)}) copy-start(f32[16,256]{1,0:T(8,128)} %filter_short.1) | copy-start | bytes 49156
  7.9 0.7 %copy-start.7 = (f32[16,256]{1,0:T(8,128)S(1)}, f32[16,256]{1,0:T(8,128)}, u32[]{:S(2)}) copy-start(f32[16,256]{1,0:T(8,128)} %filter_long.1) | copy-start | bytes 49156
  8.7 0.7 %copy-start.8 = (s32[3,512]{1,0:T(4,128)S(1)}, s32[3,512]{1,0:T(4,128)}, u32[]{:S(2)}) copy-start(s32[3,512]{1,0:T(4,128)} %wave_index.1) | copy-start | bytes 18436
  9.4 0.7 %copy-start.9 = (f32[3,256]{1,0:T(4,128)S(1)}, f32[3,256]{1,0:T(4,128)}, u32[]{:S(2)}) copy-start(f32[3,256]{1,0:T(4,128)} %positions.1) | copy-start | bytes 9220

commit v2 on v1

--- a/solution.py
+++ b/solution.py
@@ -163,11 +163,22 @@
 def kernel(
     low_count,
     high_count,
+    features_hbm,
+    positions_hbm,
+    distances_hbm,
+    pair_mask_hbm,
+    counts,
+    wave_index_hbm,
+    w_value_hbm,
+    filter_short_hbm,
+    filter_long_hbm,
+    gain_hbm,
+    w_inner_hbm,
+    w_outer_hbm,
+    updated,
     features,
-    positions,
-    distances,
-    pair_mask,
-    counts,
+    dist,
+    mask,
     wave_index,
     w_value,
     filter_short,
@@ -175,9 +186,6 @@
     gain,
     w_inner,
     w_outer,
-    updated,
-    dist,
-    mask,
     values,
     points,
     waves,
@@ -229,13 +237,28 @@
     peers += [low_peer(step) for step in range(1, low_count)]
     peers += [high_peer(step) for step in range(1, high_count)]
 
-    load_dist = pltpu.make_async_copy(distances, dist, load_sem.at[0])
-    load_mask = pltpu.make_async_copy(pair_mask, mask, load_sem.at[1])
-    load_dist.start()
-    load_mask.start()
+    sources = (
+        (features_hbm, features),
+        (w_value_hbm, w_value),
+        (positions_hbm, points.at[0]),
+        (wave_index_hbm, wave_index),
+        (filter_long_hbm, filter_long),
+        (distances_hbm, dist),
+        (pair_mask_hbm, mask),
+        (filter_short_hbm, filter_short),
+        (gain_hbm, gain),
+        (w_inner_hbm, w_inner),
+        (w_outer_hbm, w_outer),
+    )
+    loads = [
+        pltpu.make_async_copy(source, target, load_sem.at[place])
+        for place, (source, target) in enumerate(sources)
+    ]
     barrier = pltpu.get_barrier_semaphore()
     for peer in peers:
         pl.semaphore_signal(barrier, inc=1, device_id=peer, device_id_type=MESH)
+    for load in loads:
+        load.start()
 
     def remote(src, dst, send, recv, peer):
         copy = pltpu.make_async_remote_copy(
@@ -249,11 +272,12 @@
         copy.start()
         return copy
 
+    for load in loads[:4]:
+        load.wait()
     occupied = (lax.broadcasted_iota(jnp.int32, (rows, 1), 0) < counts[0]).astype(jnp.float32)
     values[1] = (
         jnp.dot(features[...], w_value[...], preferred_element_type=jnp.float32) * occupied
     ).astype(jnp.bfloat16)
-    points[0] = positions[...]
     waves[...] = jnp.zeros_like(waves)
     waves[0:3, :] = wave_index[...].astype(jnp.float32)
     pl.semaphore_wait(barrier, len(peers))
@@ -268,6 +292,7 @@
     )
     started += [points_copy, pair_copy, other_copy]
 
+    loads[4].wait()
     wave = waves[...]
     magnitude = jnp.sqrt(
         wave[0:1] * wave[0:1] + wave[1:2] * wave[1:2] + wave[2:3] * wave[2:3]
@@ -328,8 +353,8 @@
     for e in order:
         own_sums[e] = chunk_sums(((high + e) % high_count) * low_count + low)
 
-    load_dist.wait()
-    load_mask.wait()
+    for load in loads[5:]:
+        load.wait()
     turns = dist[...] * (0.5 / radius_cut)
     part = turns - jnp.floor(turns + 0.5)
     envelope[...] = (0.5 * horner(part * part, cos_terms) + 0.5) * mask[...].astype(jnp.float32)
@@ -463,17 +488,25 @@
     columns = distances.shape[1]
     bf16, f32 = jnp.bfloat16, jnp.float32
     vmem = pl.BlockSpec(memory_space=pltpu.VMEM)
-    hbm = pl.BlockSpec(memory_space=pl.ANY)
+    hbm = pl.BlockSpec(memory_space=pltpu.HBM)
     smem = pl.BlockSpec(memory_space=pltpu.SMEM)
     dma = pltpu.SemaphoreType.DMA
     return pl.pallas_call(
         functools.partial(kernel, low_count, high_count),
         out_shape=jax.ShapeDtypeStruct((rows, width), bf16),
-        in_specs=[vmem, vmem, hbm, hbm, smem] + [vmem] * 7,
+        in_specs=[hbm] * 4 + [smem] + [hbm] * 7,
         out_specs=vmem,
         scratch_shapes=[
+            pltpu.VMEM((rows, width), bf16),
             pltpu.VMEM((rows, columns), f32),
             pltpu.VMEM((rows, columns), jnp.int32),
+            pltpu.VMEM(wave_index.shape, jnp.int32),
+            pltpu.VMEM(w_value.shape, bf16),
+            pltpu.VMEM(filter_short.shape, f32),
+            pltpu.VMEM(filter_long.shape, f32),
+            pltpu.VMEM((1, width), f32),
+            pltpu.VMEM(w_inner.shape, bf16),
+            pltpu.VMEM(w_outer.shape, bf16),
             pltpu.VMEM((3, rows, width), bf16),
             pltpu.VMEM((2, 3, rows), f32),
             pltpu.VMEM((8, wave_count), f32),
@@ -492,7 +525,7 @@
             pltpu.VMEM((rows, width), f32),
             pltpu.VMEM((rows, width), bf16),
             pltpu.VMEM((rows, width), bf16),
-            dma((2,)),
+            dma((11,)),
             dma((4,)),
             dma((4,)),
             dma((low_count - 1, high_count)),
@@ -505,7 +538,7 @@
             dma((low_count - 1, high_count)),
         ],
         compiler_params=pltpu.CompilerParams(
-            collective_id=0, has_side_effects=True, vmem_limit_bytes=40 * 1024 * 1024
+            collective_id=0, has_side_effects=True, vmem_limit_bytes=63 * 1024 * 1024
         ),
         cost_estimate=pl.CostEstimate(
             flops=2 * rows * columns * width * filter_short.shape[0],

time: 43.3 us -> 35.1 us (0.81)
  local copies, waits for them, and re-layouts: 10 us -> 1.57 us
  Pallas kernels: 32.1 us -> 32.7 us
    unnamed x23 -> x1, local copies, waits for them, and re-layouts: 10 us -> 1.57 us
    pallas_call x1, Pallas kernels: 32.1 us -> 32.7 us  [kernel_body(): pl.pallas_call(functools.partial(kernel, low_count, high_count), out_shap...]
where the time goes in v2:
time: 35.1 us; the launch traced here: 35 us
  Pallas kernels  32.7 us (93%)
  local copies, waits for them, and re-layouts  1.57 us (4%)
  between operations  0.66 us (2%)
    pallas_call x1, Pallas kernels, kernel_body(): pl.pallas_call(functools.partial(kernel, low_count, high_count), out_shap...  32.7 us
    unnamed x1, local copies, waits for them, and re-layouts  1.57 us

profile of v2, /device:TPU:17, one launch (start us, length us, event | category | flops | bytes accessed | tf_op | source)
XLA Modules:
  0.0 35.0 jit_solution(6959592335320014304)
XLA Ops:
  0.7 32.7 %shard_map.118 = bf16[256,256]{1,0:T(8,128)(2,1)} custom-call(bf16[256,256]{1,0:T(8,128)(2,1)} %features_hbm.1, f32[3,256]{1,0:T(4,128)} %positions_hbm.1, f32[256,768]{1,0:T(8,128)} %distances_hbm.1, s32[256,768]{1,0:T(8,128)} %pair_mask_hbm.1, s32[1]{0:T(128)S(6)} %copy.14.counts, s32[3,512]{1,0:T(4,128)} %wave_index_hbm.1, bf16[256,256]{1,0:T(8,128)(2,1)} %w_value_hbm.1, ...), custom_call_target="tpu_custom_call" | custom-call | flops 1610612736 | bytes 1572864 | tf_op jit(solution)/shard_map/pallas_call | solution.py:494
  33.4 1.6 %copy.15 = bf16[256,256]{1,0:T(8,128)(2,1)} copy(bf16[256,256]{1,0:T(8,128)(2,1)} %shard_map.118) | data formatting | bytes 262144
